TPU v7x, 256 devices: a whole 4x4x8 slice. The times are simulated.
256 devices in a mesh: segment: 4 (over x), tok: 64 (over z, y, core).
Axes of the slice: x: 4, y: 4, z: 8, core: 2. Of those that a mesh axis runs over, the one named last changes fastest.
Arguments:
- point_feats: bfloat16 [4, 256, 64, 8, 8], P(None, ('segment', 'tok')), may hold values from -6 to 6
- point_voxel: int32 [4, 256, 64, 8], P(None, ('segment', 'tok')), may hold values from 0 to 4095
- send_counts: int32 [4, 256, 64], P(None, ('segment', 'tok')), may hold values from 0 to 8, as said below
- tok_weight: bfloat16 [2048, 512], P('segment'), may hold values from -0.125 to 0.125
- tok_gain: float32 [512], replicated, may hold values from 0.1 to 1.9
- dec_weight: bfloat16 [512, 2048], P(None, 'segment'), may hold values from -0.25 to 0.25
- dec_gain: float32 [512], replicated, may hold values from 0.1 to 1.9
- attn_gain: float32 [4, 512], P('segment'), may hold values from 0.1 to 1.9
- mlp_gain: float32 [4, 512], P('segment'), may hold values from 0.1 to 1.9
- query_gain: float32 [4, 64], P('segment'), may hold values from 0.1 to 1.9
- key_gain: float32 [4, 64], P('segment'), may hold values from 0.1 to 1.9
- qkv_weight: bfloat16 [4, 512, 1536], P('segment'), may hold values from -0.25 to 0.25
- out_weight: bfloat16 [4, 512, 512], P('segment'), may hold values from -0.25 to 0.25
- in_weight: bfloat16 [4, 512, 2048], P('segment'), may hold values from -0.25 to 0.25
- down_weight: bfloat16 [4, 2048, 512], P('segment'), may hold values from -0.125 to 0.125
Outputs:
- predictions: bfloat16 [3, 4, 1024, 2048], P(None, None, 'tok', 'segment')
Inputs may be any that keep to these rules, and one draw needn't show every extreme that they name: `send_counts`: slots past the count hold unused values. In every draw and scene some tile receives 8 points from every sender. `point_voxel`: local token of the destination tile times 256 plus the voxel within that token's patch.
All inputs are finite; a program needn't handle non-finite values.
Results may differ from a plain program's by a relative error of at most 0.03.
Values may be sent and summed in bfloat16 or wider, within the bound.
No kernel may reach another device: no remote copies, remote signals or barrier semaphores. Data moves between devices by JAX's collectives and lax.ppermute only.
A program may use at most 64 MiB of HBM per device.

v0:
```python
import math

import jax
import jax.numpy as jnp
from jax import lax
from jax.sharding import PartitionSpec as P

VOX = 256
ROLL = 3
TOK_DEV = 16


EPSILON = 1e-06


def padded(shard, sides, width):
    for axis, dim in sides:
        peers, length = (lax.axis_size(axis), shard.shape[dim])
        up = [(i, (i + 1) % peers) for i in range(peers - 1)]
        down = [(j, i) for i, j in up]
        last = lax.slice_in_dim(shard, length - width, length, axis=dim)
        first = lax.slice_in_dim(shard, 0, width, axis=dim)
        before = lax.ppermute(last, axis, up)
        after = lax.ppermute(first, axis, down)
        shard = jnp.concatenate([before, shard, after], axis=dim)
    return shard


def from_behind(block, axis, distance):
    devices = range(lax.axis_size(axis))
    route = [(i - distance, i) for i in devices if i - distance in devices]
    return lax.ppermute(block, axis, route)


def spread_2(block, axis, owner):
    block = jnp.where(lax.axis_index(axis) == owner, block, jnp.zeros_like(block))
    return lax.psum(block, axis)


def rms_scale(tensor, factor):
    return tensor * lax.rsqrt(jnp.mean(tensor * tensor, axis=-1, keepdims=True) + EPSILON) * factor


def head_scale(tensor, factor, heads):
    shaped = tensor.reshape(tensor.shape[:-1] + (heads, tensor.shape[-1] // heads))
    return rms_scale(shaped, factor)


def band_gate(tok_rows, tok_rank, tok_count):
    query_pos = tok_rank * tok_rows + jnp.arange(tok_rows)
    key_pos = (tok_rank - 1) * tok_rows + jnp.arange(3 * tok_rows)
    near = jnp.abs(query_pos[:, None] - key_pos[None, :]) <= tok_rows
    inside = (key_pos >= 0) & (key_pos < tok_rows * tok_count)
    return (near & inside[None, :]).astype(jnp.float32)


def project(tensor, weight):
    return jnp.einsum("gtd,de->gte", tensor, weight, preferred_element_type=jnp.float32)


def split_heads(tensor, heads):
    return tensor.reshape(tensor.shape[:-1] + (heads, tensor.shape[-1] // heads))


def attend(queries, key_rows, value_rows, gate):
    head_dim = queries.shape[-1]
    scores = jnp.einsum(
        "gqhd,gkhd->ghqk", queries, key_rows, preferred_element_type=jnp.float32
    ) / math.sqrt(head_dim)
    weights = jnp.exp(scores) * gate
    attn_probs = (weights / jnp.sum(weights, axis=-1, keepdims=True)).astype(jnp.bfloat16)
    blended = jnp.einsum(
        "ghqk,gkhd->gqhd", attn_probs, value_rows, preferred_element_type=jnp.float32
    )
    return blended.astype(jnp.bfloat16)


def one_layer(stream, layer_no, params, gate):
    attn_gain, mlp_gain, query_gain, key_gain, qkv_weight, out_weight, in_weight, down_weight = (
        params
    )
    groups, tok_rows, width = stream.shape
    heads = width // query_gain.shape[-1]
    normed = rms_scale(stream, attn_gain[layer_no]).astype(jnp.bfloat16)
    own_proj = project(normed, qkv_weight[layer_no])
    queries = head_scale(own_proj[..., :width], query_gain[layer_no], heads).astype(jnp.bfloat16)
    own_keys = head_scale(own_proj[..., width : 2 * width], key_gain[layer_no], heads).astype(
        jnp.bfloat16
    )
    own_keys = own_keys.reshape(groups, tok_rows, width)
    own_values = own_proj[..., 2 * width :].astype(jnp.bfloat16)
    paired = jnp.concatenate([own_keys, own_values], axis=-1)
    spread = padded(paired, (("tok", 1),), tok_rows)
    key_rows = spread[..., :width]
    value_rows = spread[..., width:]
    blended = attend(queries, split_heads(key_rows, heads), split_heads(value_rows, heads), gate)
    attended = stream + project(blended.reshape(groups, tok_rows, width), out_weight[layer_no])
    normed_ff = rms_scale(attended, mlp_gain[layer_no]).astype(jnp.bfloat16)
    hidden = jax.nn.gelu(project(normed_ff, in_weight[layer_no])).astype(jnp.bfloat16)
    return attended + project(hidden, down_weight[layer_no])


def run_section(entering, params, gate):
    layer_out = entering
    layer_out = one_layer(layer_out, 0, params, gate)
    return layer_out


def tokenize(partial_value, tok_gain):
    summed = lax.psum(partial_value, "segment")
    return rms_scale(summed, tok_gain).astype(jnp.bfloat16)


def handoff(leaving):
    return from_behind(leaving, "segment", 1)


def decode_frame(leaving, dec_gain, dec_weight, tok_weight, tok_gain, wanted):
    last_out = spread_2(leaving, "segment", lax.axis_size("segment") - 1)
    normed_dec = rms_scale(last_out, dec_gain).astype(jnp.bfloat16)
    predicted = jnp.tanh(project(normed_dec, dec_weight)).astype(jnp.bfloat16)
    if wanted:
        return (predicted, tokenize(project(predicted, tok_weight), tok_gain))
    return (predicted, None)


def scatter_points(point_feats, point_voxel, send_counts, tok_weight):
    slot_total = point_feats.shape[3]
    live_slot = jnp.arange(slot_total)[None, None, None, :] < send_counts[..., None]
    masked = jnp.where(live_slot[..., None], point_feats, jnp.zeros_like(point_feats))
    features, voxels = (
        lax.all_to_all(masked, "tok", split_axis=2, concat_axis=1, tiled=True),
        lax.all_to_all(point_voxel, "tok", split_axis=2, concat_axis=1, tiled=True),
    )
    sections = lax.axis_size("segment")
    height_part = VOX // sections
    scenes = features.shape[0]
    channels = features.shape[-1]
    features = features.reshape(scenes, -1, channels)
    voxels = voxels.reshape(scenes, -1)
    within = voxels % VOX
    column = within // height_part * TOK_DEV + voxels // VOX
    pick_cell = (column[..., None] == jnp.arange(sections * TOK_DEV)).astype(jnp.bfloat16)
    pick_voxel = ((within % height_part)[..., None] == jnp.arange(height_part)).astype(jnp.bfloat16)
    weighted = features[:, :, :, None] * pick_cell[:, :, None, :]
    voxel_grid = jnp.einsum(
        "srem,sru->smeu", weighted, pick_voxel, preferred_element_type=jnp.float32
    )
    voxel_grid = voxel_grid.reshape(scenes, sections, TOK_DEV, channels * height_part)
    mine = lax.psum_scatter(voxel_grid, "segment", scatter_dimension=1, tiled=True)[:, 0]
    return project(mine.astype(jnp.bfloat16), tok_weight)


def local(
    point_feats,
    point_voxel,
    send_counts,
    tok_weight,
    tok_gain,
    dec_weight,
    dec_gain,
    attn_gain,
    mlp_gain,
    query_gain,
    key_gain,
    qkv_weight,
    out_weight,
    in_weight,
    down_weight,
):
    sections = lax.axis_size("segment")
    first = lax.axis_index("segment") == 0
    gate = band_gate(TOK_DEV, lax.axis_index("tok"), lax.axis_size("tok"))
    params = (
        attn_gain,
        mlp_gain,
        query_gain,
        key_gain,
        qkv_weight,
        out_weight,
        in_weight,
        down_weight,
    )
    opening = tokenize(
        scatter_points(point_feats, point_voxel, send_counts, tok_weight), tok_gain
    ).astype(jnp.float32)
    frames = []
    frame_input = opening
    carried = opening
    for frame_index in range(ROLL):
        for section in range(sections):
            entering = jnp.where(first, frame_input, carried)
            leaving = run_section(entering, params, gate)
            carried = handoff(leaving)
        predicted, upcoming = decode_frame(
            leaving, dec_gain, dec_weight, tok_weight, tok_gain, frame_index + 1 < ROLL
        )
        frames.append(predicted)
        if upcoming is not None:
            frame_input = upcoming.astype(jnp.float32)
    return jnp.stack(frames)


def solution(mesh):
    return jax.shard_map(
        local,
        mesh=mesh,
        in_specs=(
            P(None, ("segment", "tok"), None, None, None),
            P(None, ("segment", "tok"), None, None),
            P(None, ("segment", "tok"), None),
            P("segment", None),
            P(),
            P(None, "segment"),
            P(),
            P("segment", None),
            P("segment", None),
            P("segment", None),
            P("segment", None),
            P("segment", None, None),
            P("segment", None, None),
            P("segment", None, None),
            P("segment", None, None),
        ),
        out_specs=P(None, None, "tok", "segment"),
        check_vma=False,
    )
```

profile of v0, /device:TPU:8, one launch (start us, length us, event | category | flops | bytes accessed | tf_op | source)
XLA Modules:
  0.0 847.7 jit_solution(12562325053258205435)
XLA Ops:
  8.2 12.1 %all-to-all-start = ((s32[4,1,64,8]{3,0,1,2:T(4,128)}), s32[4,1,64,8]{3,0,1,2:T(4,128)S(1)}, u32[]{:S(2)}, u32[]{:S(2)}) async-start(s32[4,1,64,8]{3,0,1,2:T(4,128)} %copy.240), calls=%async_computation | async-start | bytes 262144 | tf_op jit(solution)/shard_map/all_to_all | solution.py:133
  25.8 4.4 all-to-all-done
  30.2 5.9 all-to-all-start.1
  36.4 8.3 all-to-all-done.1
  53.2 22.9 %all-reduce.20 = bf16[4,4,16,512]{3,2,1,0:T(8,128)(2,1)S(1)} all-reduce(f32[4,4,16,512]{3,2,1,0:T(8,128)S(1)} %reshape.826), channel_id=2, replica_groups=mesh['segment'=4,'tok'=64] {'segment'}, use_global_device_ids=true, to_apply=%region_0.1.clone | all-reduce | flops 131072 | bytes 786432
  77.7 40.2 %all-reduce.9.cloned.1.call-done = f32[4,16,512]{2,1,0:T(8,128)} async-done(((f32[4,16,512]{2,1,0:T(8,128)}), f32[4,16,512]{2,1,0:T(8,128)}) %all-reduce.9.cloned.1.call-update) | async-done | bytes 131088 | tf_op jit(solution)/shard_map/psum | solution.py:110
  127.5 3.6 collective-permute-start.1
  147.8 3.0 collective-permute-done.2
  161.4 2.9 collective-permute-start.3
  164.3 2.9 collective-permute-start.4
  181.1 3.2 fusion.116
  184.3 4.4 collective-permute-start.5
  188.7 3.1 collective-permute-done.5
  202.3 3.1 collective-permute-start.6
  222.0 3.2 fusion.119
  225.2 4.3 collective-permute-start.8
  229.4 2.8 collective-permute-done.8
  242.8 2.9 collective-permute-start.10
  263.6 3.2 broadcast_select_fusion.1
  266.9 61.8 %all-reduce.11.cloned.1.call-done = f32[4,16,512]{2,1,0:T(8,128)} async-done(((f32[4,16,512]{2,1,0:T(8,128)}), f32[4,16,512]{2,1,0:T(8,128)}) %all-reduce.11.cloned.1.call-update) | async-done | bytes 131088 | tf_op jit(solution)/shard_map/psum | solution.py:37
  334.9 44.6 %all-reduce.13.cloned.1.call-done = f32[4,16,512]{2,1,0:T(8,128)} async-done(((f32[4,16,512]{2,1,0:T(8,128)}), f32[4,16,512]{2,1,0:T(8,128)}) %all-reduce.13.cloned.1.call-update) | async-done | bytes 131088 | tf_op jit(solution)/shard_map/psum | solution.py:110
  394.0 3.9 collective-permute-start.13
  411.8 3.2 fusion.125
  417.2 3.6 collective-permute-done.14
  434.0 2.9 collective-permute-start.16
  451.0 3.2 fusion.128
  454.1 4.3 collective-permute-start.17
  458.4 3.1 collective-permute-done.17
  472.0 3.1 collective-permute-start.18
  491.7 3.2 fusion.131
  494.9 4.3 collective-permute-start.20
  499.1 2.8 collective-permute-done.20
  512.5 4.0 collective-permute-start.21
  532.7 3.2 broadcast_select_fusion
  536.0 60.6 %all-reduce.15.cloned.1.call-done = f32[4,16,512]{2,1,0:T(8,128)} async-done(((f32[4,16,512]{2,1,0:T(8,128)}), f32[4,16,512]{2,1,0:T(8,128)}) %all-reduce.15.cloned.1.call-update) | async-done | bytes 131088 | tf_op jit(solution)/shard_map/psum | solution.py:37
  602.2 44.6 %all-reduce.17.cloned.1.call-done = f32[4,16,512]{2,1,0:T(8,128)} async-done(((f32[4,16,512]{2,1,0:T(8,128)}), f32[4,16,512]{2,1,0:T(8,128)}) %all-reduce.17.cloned.1.call-update) | async-done | bytes 131088 | tf_op jit(solution)/shard_map/psum | solution.py:110
  658.8 3.6 collective-permute-start.25
  677.8 3.1 collective-permute-done.26
  689.0 2.7 collective-permute-start.27
  691.8 2.8 collective-permute-start.28
  707.7 4.4 collective-permute-start.29
  712.1 2.8 collective-permute-done.29
  723.0 3.1 collective-permute-start.30
  726.1 2.7 collective-permute-start.31
  741.7 4.4 collective-permute-start.32
  756.6 3.9 collective-permute-start.33
  773.1 3.2 fusion.149
  776.3 61.1 %all-reduce.19.cloned.1.call-done = f32[4,16,512]{2,1,0:T(8,128)} async-done(((f32[4,16,512]{2,1,0:T(8,128)}), f32[4,16,512]{2,1,0:T(8,128)}) %all-reduce.19.cloned.1.call-update) | async-done | bytes 131088 | tf_op jit(solution)/shard_map/psum | solution.py:37
  (530 shorter events, 341.2 us)
Async XLA Ops:
  6.5 136.5 %copy-start = (bf16[1,2048,512]{2,1,0:T(8,128)(2,1)S(1)}, bf16[1,2048,512]{2,1,0:T(8,128)(2,1)}, u32[]{:S(2)}) copy-start(bf16[1,2048,512]{2,1,0:T(8,128)(2,1)} %param.29) | copy-start | bytes 6291460
  8.2 22.1 %all-to-all-start = ((s32[4,1,64,8]{3,0,1,2:T(4,128)}), s32[4,1,64,8]{3,0,1,2:T(4,128)S(1)}, u32[]{:S(2)}, u32[]{:S(2)}) async-start(s32[4,1,64,8]{3,0,1,2:T(4,128)} %copy.240), calls=%async_computation | async-start | bytes 262144 | tf_op jit(solution)/shard_map/all_to_all | solution.py:133
  30.2 14.4 %all-to-all-start.1 = ((bf16[64,2,128]{2,1,0:T(2,128)(2,1)}), bf16[64,2,128]{2,1,0:T(2,128)(2,1)S(1)}, u32[]{:S(2)}, u32[]{:S(2)}) async-start(bf16[64,2,128]{2,1,0:T(2,128)(2,1)} %reshape.885), calls=%async_computation.1 | async-start | bytes 65536 | tf_op jit(solution)/shard_map/all_to_all | solution.py:132
  36.1 81.8 %all-reduce.9.cloned.1.call-start = ((), (), s32[]{:S(2)}) async-start(), calls=%async_computation.2 | async-start | bytes 262144 | tf_op jit(solution)/shard_map/psum | solution.py:110
  77.6 251.1 %all-reduce.11.cloned.1.call-start = ((), (), s32[]{:S(2)}) async-start(), calls=%async_computation.3 | async-start | bytes 262144 | tf_op jit(solution)/shard_map/psum | solution.py:37
  125.6 6.7 collective-permute-start
  127.5 6.2 collective-permute-start.1
  145.6 5.3 collective-permute-start.2
  161.4 8.4 collective-permute-start.3
  164.3 5.5 collective-permute-start.4
  184.3 7.5 collective-permute-start.5
  202.3 8.2 collective-permute-start.6
  205.4 5.3 collective-permute-start.7
  225.2 7.1 collective-permute-start.8
  242.8 8.2 collective-permute-start.10
  245.7 6.6 collective-permute-start.9
  263.6 116.9 %copy-start.55 = (f32[512]{0:T(512)S(1)}, f32[512]{0:T(512)}, u32[]{:S(2)}) copy-start(f32[512]{0:T(512)} %param.19) | copy-start | bytes 6148
  266.8 114.8 %copy-start.45 = (f32[1,512]{1,0:T(1,128)S(1)}, f32[1,512]{1,0:T(1,128)}, u32[]{:S(2)}) copy-start(f32[1,512]{1,0:T(1,128)} %param.22) | copy-start | bytes 6148
  266.9 112.6 %all-reduce.13.cloned.1.call-start = ((), (), s32[]{:S(2)}) async-start(), calls=%async_computation.4 | async-start | bytes 262144 | tf_op jit(solution)/shard_map/psum | solution.py:110
  332.6 264.0 %all-reduce.15.cloned.1.call-start = ((), (), s32[]{:S(2)}) async-start(), calls=%async_computation.5 | async-start | bytes 262144 | tf_op jit(solution)/shard_map/psum | solution.py:37
  332.6 47.8 %collective-permute-start.11 = (f32[4,16,512]{2,1,0:T(8,128)}, f32[4,16,512]{2,1,0:T(8,128)S(1)}, u32[]{:S(2)}, u32[]{:S(2)}) collective-permute-start(f32[4,16,512]{2,1,0:T(8,128)} %get-tuple-element.70), channel_id=1, source_target_pairs={{0,64},{64,128},{128,192},{1,65},{65,129},{129,193},{2,66},{66,130... | collective-permute-start | bytes 393224 | tf_op jit(solution)/shard_map/ppermute | solution.py:32
  392.1 8.4 collective-permute-start.12
  394.0 6.5 collective-permute-start.13
  415.0 5.8 collective-permute-start.14
  431.3 8.2 collective-permute-start.15
  434.0 5.7 collective-permute-start.16
  454.1 7.3 collective-permute-start.17
  472.0 8.2 collective-permute-start.18
  475.2 5.2 collective-permute-start.19
  494.9 7.1 collective-permute-start.20
  512.5 8.9 %collective-permute-start.21 = (bf16[4,16,1024]{2,1,0:T(8,128)(2,1)}, bf16[4,16,1024]{2,1,0:T(8,128)(2,1)}, u32[]{:S(2)}, u32[]{:S(2)}) collective-permute-start(bf16[4,16,1024]{2,1,0:T(8,128)(2,1)} %pad_maximum_fusion.20), channel_id=1, source_target_pairs={{0,1},{1,2},{2,3},{3,4},{4,5},{5,6},{6,7},{7,8},{8,9},{9,10},{10,1... | collective-permute-start | bytes 393224 | tf_op jit(solution)/shard_map/ppermute | solution.py:23
  516.5 4.8 collective-permute-start.22
  532.7 115.1 %copy-start.56 = (f32[512]{0:T(512)S(1)}, f32[512]{0:T(512)}, u32[]{:S(2)}) copy-start(f32[512]{0:T(512)} %param.19) | copy-start | bytes 6148
  535.9 113.0 %copy-start.49 = (f32[1,512]{1,0:T(1,128)S(1)}, f32[1,512]{1,0:T(1,128)}, u32[]{:S(2)}) copy-start(f32[1,512]{1,0:T(1,128)} %param.22) | copy-start | bytes 6148
  535.9 110.8 %all-reduce.17.cloned.1.call-start = ((), (), s32[]{:S(2)}) async-start(), calls=%async_computation.6 | async-start | bytes 262144 | tf_op jit(solution)/shard_map/psum | solution.py:110
  599.9 237.6 %all-reduce.19.cloned.1.call-start = ((), (), s32[]{:S(2)}) async-start(), calls=%async_computation.7 | async-start | bytes 262144 | tf_op jit(solution)/shard_map/psum | solution.py:37
  599.9 47.8 %collective-permute-start.23 = (f32[4,16,512]{2,1,0:T(8,128)}, f32[4,16,512]{2,1,0:T(8,128)S(1)}, u32[]{:S(2)}, u32[]{:S(2)}) collective-permute-start(f32[4,16,512]{2,1,0:T(8,128)} %get-tuple-element.80), channel_id=1, source_target_pairs={{0,64},{64,128},{128,192},{1,65},{65,129},{129,193},{2,66},{66,130... | collective-permute-start | bytes 393224 | tf_op jit(solution)/shard_map/ppermute | solution.py:32
  656.8 7.3 collective-permute-start.24
  658.8 6.5 collective-permute-start.25
  675.5 5.4 collective-permute-start.26
  689.0 7.3 collective-permute-start.27
  691.8 5.6 collective-permute-start.28
  707.7 7.2 collective-permute-start.29
  723.0 7.6 collective-permute-start.30
  726.1 5.3 collective-permute-start.31
  741.7 6.9 collective-permute-start.32
  756.6 7.5 collective-permute-start.33
  760.5 4.7 collective-permute-start.34
  (55 other events, 863.5 us)
Sparse Core Ops, SparseCore 0:
  77.7 40.1 all-reduce.8
  267.0 61.6 all-reduce.10
  332.7 46.7 all-reduce.12
  536.1 60.5 all-reduce.14
  600.0 46.7 all-reduce.16
  776.4 60.9 all-reduce.18
where the time goes:
time: 861 us; the launch traced here: 848 us
  waiting for transfers between devices  360 us (42%)
  starting transfers between devices  124 us (14%)
  local copies, waits for them, and re-layouts  123 us (14%)
  matrix products  117 us (14%)
  other arithmetic  85.5 us (10%)
  blocking collectives  22.9 us (3%)
  between operations  16 us (2%)
    psum x3, waiting for transfers between devices, spread_2(): return lax.psum(block, axis)  184 us
    psum x3, waiting for transfers between devices, tokenize(): summed = lax.psum(partial_value, 'segment')  129 us
    dot_general x42, matrix products, project(): jnp.einsum('gtd,de->gte', tensor, weight, preferred_element_type=jnp.floa...  68.4 us
    reshape x24, local copies, waits for them, and re-layouts, split_heads(): tensor.reshape(tensor.shape[:-1] + (heads, tensor.shape[-1] // heads))  38.4 us
    ppermute x11, starting transfers between devices, from_behind(): return lax.ppermute(block, axis, route)  37.3 us
    ppermute x12, starting transfers between devices, padded(): after = lax.ppermute(first, axis, down)  34.4 us
    ppermute x12, starting transfers between devices, padded(): before = lax.ppermute(last, axis, up)  33.8 us
    mul x26, local copies, waits for them, and re-layouts, rms_scale(): tensor * lax.rsqrt(jnp.mean(tensor * tensor, axis=-1, keepdims=True) + EP...  29.7 us
  transfers between devices with their start and end apart: 43, of which 26 were waited for; matrix products, arithmetic and copies ran while one was open for 4% of the time, Pallas kernels for 0%

commit v1 on v0

v1 whole, which is shorter than its diff:
```python
import functools

import jax
import jax.numpy as jnp
from jax import lax
from jax.experimental import pallas as pl
from jax.experimental.pallas import tpu as pltpu
from jax.sharding import PartitionSpec as P

LAYERS = 4
ROLL = 3
TOK_DEV = 16
TILES = 64
TOKENS = TILES * TOK_DEV
WIDTH = 512
HEADS = 8
HEAD_DIM = 64
SECTIONS = 4
SLOTS = 8
CHANNELS = 8
HALO = LAYERS
EPSILON = 1e-06

F32 = jnp.float32
BF16 = jnp.bfloat16

QKV, OUT, IN, DOWN, DEC, TOK = range(6)
WEIGHT_ROWS = (512, 512, 512, 2048, 512, 512)
WEIGHT_COLS = (1536, 512, 2048, 512, 512, 512)


def rms_scale(tensor, factor):
    return tensor * lax.rsqrt(jnp.mean(tensor * tensor, axis=-1, keepdims=True) + EPSILON) * factor


def dot(left, right):
    return jnp.dot(left, right, preferred_element_type=F32)


def dot_t(left, right):
    return lax.dot_general(left, right, (((1,), (1,)), ((), ())), preferred_element_type=F32)


def low_lanes(shape):
    return lax.broadcasted_iota(jnp.int32, shape, 1) % 128 < HEAD_DIM


def head_scale(tensor, factor, pool):
    parts = []
    for start in range(0, WIDTH, 256):
        part = tensor[:, start : start + 256]
        mean = dot((part * part).astype(BF16), pool)
        parts.append(part * lax.rsqrt(mean + EPSILON))
    return (jnp.concatenate(parts, axis=1) * factor).astype(BF16)


def attention(queries, key_rows, value_rows, near):
    rows = queries.shape[0]
    low = low_lanes((rows, 128))
    zero = jnp.zeros((rows, 128), BF16)
    outs = []
    for pair in range(HEADS // 2):
        cols = slice(128 * pair, 128 * pair + 128)
        both = queries[:, cols]
        stacked = jnp.concatenate([jnp.where(low, both, zero), jnp.where(low, zero, both)], axis=0)
        weights = jnp.where(near, jnp.exp(dot_t(stacked, key_rows[:, cols])), 0.0)
        total = jnp.maximum(jnp.sum(weights, axis=-1, keepdims=True), 1e-30)
        probs = (weights / total).astype(BF16)
        mixed = dot(probs, value_rows[:, cols])
        outs.append(jnp.where(low, mixed[:rows], mixed[rows:]))
    return jnp.concatenate(outs, axis=1).astype(BF16)


def near_mask(tile, halo, rows, keys):
    query = lax.broadcasted_iota(jnp.int32, (2 * rows, keys), 0) % rows + TOK_DEV
    key = lax.broadcasted_iota(jnp.int32, (2 * rows, keys), 1)
    position = (tile - halo) * TOK_DEV + key
    return (jnp.abs(query - key) <= TOK_DEV) & (position >= 0) & (position < TOKENS)


def frame_kernel(with_next, *refs):
    (tile_ref, x_ref, gains_ref, heads_ref, dec_gain_ref, tok_gain_ref), refs = refs[:6], refs[6:]
    halves, refs = refs[:12], refs[12:]
    if with_next:
        (pred_ref, next_ref), refs = refs[:2], refs[2:]
    else:
        (pred_ref,), refs = refs[:1], refs[1:]
    slots, sems = refs[:6], refs[6]
    tile = tile_ref[0]
    core = tile % 2

    def copies(kind, index):
        half = WEIGHT_COLS[kind] // 2
        rows = WEIGHT_ROWS[kind]
        made = []
        for side in range(2):
            column = jnp.where(side == 0, core, 1 - core) * half
            if kind in (DEC, TOK):
                column = column + (index * 512 if kind == DEC else 0)
                place = slots[kind].at[
                    pl.ds(index * rows if kind == TOK else 0, rows),
                    pl.ds(pl.multiple_of(column, 128), half),
                ]
            else:
                place = slots[kind].at[index, :, pl.ds(pl.multiple_of(column, 128), half)]
            made.append(
                pltpu.make_async_copy(
                    halves[2 * kind + side].at[pl.ds(index * rows, rows), :],
                    place,
                    sems.at[kind, index, side],
                )
            )
        return made

    def begin(kind, index):
        for copy in copies(kind, index):
            copy.start()

    def ready(kind, index):
        for copy in copies(kind, index):
            copy.wait()

    for layer in range(LAYERS):
        for kind in (QKV, OUT, IN, DOWN):
            begin(kind, layer)
    for kind in (DEC, TOK) if with_next else (DEC,):
        for section in range(SECTIONS):
            begin(kind, section)

    row = lax.broadcasted_iota(jnp.int32, (256, 256), 0) // HEAD_DIM
    col = lax.broadcasted_iota(jnp.int32, (256, 256), 1) // HEAD_DIM
    pool = jnp.where(row == col, 1.0 / HEAD_DIM, 0.0).astype(BF16)

    stream = x_ref[...].astype(F32)
    for layer in range(LAYERS):
        halo = LAYERS - layer
        keys = (2 * halo + 1) * TOK_DEV
        rows = keys - 2 * TOK_DEV
        own = slice(TOK_DEV, TOK_DEV + rows)
        normed = rms_scale(stream, gains_ref[layer : layer + 1, :]).astype(BF16)
        ready(QKV, layer)
        projected = dot(normed, slots[QKV][layer])
        queries = head_scale(projected[own, :WIDTH], heads_ref[layer : layer + 1, :], pool)
        key_rows = head_scale(
            projected[:, WIDTH : 2 * WIDTH], heads_ref[LAYERS + layer : LAYERS + layer + 1, :], pool
        )
        value_rows = projected[:, 2 * WIDTH :].astype(BF16)
        blended = attention(queries, key_rows, value_rows, near_mask(tile, halo, rows, keys))
        ready(OUT, layer)
        attended = stream[own] + dot(blended, slots[OUT][layer])
        normed_ff = rms_scale(attended, gains_ref[LAYERS + layer : LAYERS + layer + 1, :])
        ready(IN, layer)
        hidden = jax.nn.gelu(dot(normed_ff.astype(BF16), slots[IN][layer])).astype(BF16)
        ready(DOWN, layer)
        stream = attended + dot(hidden, slots[DOWN][layer])

    normed_dec = rms_scale(stream, dec_gain_ref[...]).astype(BF16)
    for section in range(SECTIONS):
        ready(DEC, section)
    predicted = jnp.tanh(dot(normed_dec, slots[DEC][...])).astype(BF16)
    for section in range(SECTIONS):
        pred_ref[section] = predicted[:, section * 512 : section * 512 + 512]
    if with_next:
        for section in range(SECTIONS):
            ready(TOK, section)
        upcoming = rms_scale(dot(predicted, slots[TOK][...]), tok_gain_ref[...])
        next_ref[...] = upcoming.astype(BF16)


def frame(tile, rows, gains, head_gains, dec_gain, tok_gain, halves, with_next):
    vmem = pl.BlockSpec(memory_space=pltpu.VMEM)
    out_shape = [jax.ShapeDtypeStruct((SECTIONS, TOK_DEV, 512), BF16)]
    if with_next:
        out_shape.append(jax.ShapeDtypeStruct((TOK_DEV, WIDTH), BF16))
    return pl.pallas_call(
        functools.partial(frame_kernel, with_next),
        out_shape=out_shape,
        in_specs=[pl.BlockSpec(memory_space=pltpu.SMEM)]
        + [vmem] * 5
        + [pl.BlockSpec(memory_space=pl.ANY)] * 12,
        out_specs=[vmem] * len(out_shape),
        scratch_shapes=[
            pltpu.VMEM((LAYERS, 512, 1536), BF16),
            pltpu.VMEM((LAYERS, 512, 512), BF16),
            pltpu.VMEM((LAYERS, 512, 2048), BF16),
            pltpu.VMEM((LAYERS, 2048, 512), BF16),
            pltpu.VMEM((512, 2048), BF16),
            pltpu.VMEM((2048, 512), BF16),
            pltpu.SemaphoreType.DMA((6, 4, 2)),
        ],
        compiler_params=pltpu.CompilerParams(vmem_limit_bytes=52 * 1024 * 1024),
        name="frame",
    )(tile, rows, gains, head_gains, dec_gain, tok_gain, *halves)


def scatter_kernel(tile_ref, points_ref, tok_gain_ref, mine_ref, other_ref, out_ref, tok_ref, sems):
    core = tile_ref[0] % 2

    def copies():
        return [
            pltpu.make_async_copy(
                half_ref,
                tok_ref.at[:, pl.ds(pl.multiple_of(column * 256, 128), 256)],
                sems.at[side],
            )
            for side, (half_ref, column) in enumerate(((mine_ref, core), (other_ref, 1 - core)))
        ]

    for copy in copies():
        copy.start()
    turned = jnp.transpose(points_ref[...].astype(F32))
    senders = turned.shape[1]
    cell_ids = lax.broadcasted_iota(jnp.int32, (64, senders), 0).astype(F32)
    voxel_ids = (lax.broadcasted_iota(jnp.int32, (128, senders), 0) % 64).astype(F32)
    totals = jnp.zeros((CHANNELS * 64, 128), F32)
    for slot in range(SLOTS):
        cell = turned[64 + slot : 65 + slot, :]
        voxel = turned[72 + slot : 73 + slot, :]
        here = cell_ids == cell
        picked = jnp.where(voxel_ids == voxel, 1.0, 0.0).astype(BF16)
        weighted = jnp.concatenate(
            [
                jnp.where(here, turned[slot * CHANNELS + e : slot * CHANNELS + e + 1, :], 0.0)
                for e in range(CHANNELS)
            ],
            axis=0,
        ).astype(BF16)
        totals = totals + dot_t(weighted, picked)
    low = low_lanes((TOK_DEV, 128))
    columns = []
    for section in range(SECTIONS):
        for e in range(0, CHANNELS, 2):
            first = e * 64 + section * TOK_DEV
            second = first + 64
            columns.append(
                jnp.where(low, totals[first : first + TOK_DEV], totals[second : second + TOK_DEV])
            )
    grid = jnp.concatenate(columns, axis=1).astype(BF16)
    for copy in copies():
        copy.wait()
    out_ref[...] = rms_scale(dot(grid, tok_ref[...]), tok_gain_ref[...]).astype(BF16)


def scatter(tile, points, tok_gain, mine, other):
    vmem = pl.BlockSpec(memory_space=pltpu.VMEM)
    return pl.pallas_call(
        scatter_kernel,
        out_shape=jax.ShapeDtypeStruct((TOK_DEV, WIDTH), BF16),
        in_specs=[pl.BlockSpec(memory_space=pltpu.SMEM), vmem, vmem]
        + [pl.BlockSpec(memory_space=pl.ANY)] * 2,
        out_specs=vmem,
        scratch_shapes=[pltpu.VMEM((2048, 512), BF16), pltpu.SemaphoreType.DMA((2,))],
        compiler_params=pltpu.CompilerParams(vmem_limit_bytes=32 * 1024 * 1024),
        name="scatter",
    )(tile, points, tok_gain, mine, other)


def sibling(block):
    return lax.ppermute(block, "tok", [(i, i ^ 1) for i in range(TILES)])


def gather_half(weight):
    tile = lax.axis_index("tok")
    rows, cols = weight.shape
    piece = lax.dynamic_slice(
        weight, (tile // 2 * (rows // 32), tile % 2 * (cols // 2)), (rows // 32, cols // 2)
    )
    groups = [
        [s * TILES + zy * 2 + core for s in range(SECTIONS) for zy in range(TILES // 2)]
        for core in range(2)
    ]
    return lax.all_gather(piece, ("segment", "tok"), axis_index_groups=groups, tiled=True)


def with_halo(block):
    blocks = []
    for shift in range(-HALO, HALO + 1):
        if shift == 0:
            blocks.append(block)
        else:
            route = [(i + shift, i) for i in range(TILES) if 0 <= i + shift < TILES]
            blocks.append(lax.ppermute(block, "tok", route))
    return jnp.concatenate(blocks, axis=0)


def send_points(point_feats, point_voxel, send_counts):
    feats = point_feats.reshape(SECTIONS * TILES, SLOTS * CHANNELS)
    voxel = point_voxel.reshape(SECTIONS * TILES, SLOTS)
    counts = send_counts.reshape(SECTIONS * TILES, 1)
    live = jnp.arange(SLOTS)[None, :] < counts
    cell = jnp.where(live, voxel // 64 % SECTIONS * TOK_DEV + voxel // 256, -1).astype(BF16)
    inner = (voxel % 64).astype(BF16)
    message = jnp.concatenate(
        [feats, cell, inner, jnp.zeros((SECTIONS * TILES, 48), BF16)], axis=1
    )
    return lax.all_to_all(message, ("segment", "tok"), split_axis=0, concat_axis=0, tiled=True)


def local(
    point_feats,
    point_voxel,
    send_counts,
    tok_weight,
    tok_gain,
    dec_weight,
    dec_gain,
    attn_gain,
    mlp_gain,
    query_gain,
    key_gain,
    qkv_weight,
    out_weight,
    in_weight,
    down_weight,
):
    tile = lax.axis_index("tok").astype(jnp.int32).reshape(1)
    points = send_points(point_feats, point_voxel, send_counts)
    own_gains = jnp.concatenate([attn_gain, mlp_gain, query_gain, key_gain], axis=1)
    all_gains = lax.all_to_all(
        jnp.broadcast_to(own_gains, (SECTIONS, own_gains.shape[1])),
        "segment",
        split_axis=0,
        concat_axis=0,
        tiled=True,
    )
    gains = jnp.concatenate([all_gains[:, :512], all_gains[:, 512:1024]], axis=0)
    head_gains = jnp.concatenate(
        [
            jnp.tile(all_gains[:, 1024:1088], (1, HEADS)) * 0.125,
            jnp.tile(all_gains[:, 1088:], (1, HEADS)),
        ],
        axis=0,
    )
    halves = []
    for weight in (qkv_weight[0], out_weight[0], in_weight[0], down_weight[0], dec_weight, tok_weight):
        mine = gather_half(weight)
        halves += [mine, sibling(mine)]
    tok_gain = tok_gain[None]
    dec_gain = dec_gain[None]
    entering = scatter(tile, points, tok_gain, halves[10], halves[11])
    frames = []
    for frame_index in range(ROLL):
        with_next = frame_index + 1 < ROLL
        made = frame(
            tile,
            with_halo(entering),
            gains,
            head_gains,
            dec_gain,
            tok_gain,
            halves,
            with_next,
        )
        frames.append(
            lax.all_to_all(made[0], "segment", split_axis=0, concat_axis=0, tiled=True)
        )
        if with_next:
            entering = made[1]
    return jnp.stack(frames)


def solution(mesh):
    return jax.shard_map(
        local,
        mesh=mesh,
        in_specs=(
            P(None, ("segment", "tok"), None, None, None),
            P(None, ("segment", "tok"), None, None),
            P(None, ("segment", "tok"), None),
            P("segment", None),
            P(),
            P(None, "segment"),
            P(),
            P("segment", None),
            P("segment", None),
            P("segment", None),
            P("segment", None),
            P("segment", None, None),
            P("segment", None, None),
            P("segment", None, None),
            P("segment", None, None),
        ),
        out_specs=P(None, None, "tok", "segment"),
        check_vma=False,
    )
```

time: 861 us -> 806 us (0.936)
  waiting for transfers between devices: 360 us -> 614 us
  matrix products: 117 us -> 0 us
  local copies, waits for them, and re-layouts: 123 us -> 16.4 us
  other arithmetic: 85.5 us -> 2.22 us
  starting transfers between devices: 124 us -> 71.5 us
  Pallas kernels: 0 us -> 41.2 us
  blocking collectives: 22.9 us -> 41.1 us
    all_gather x0 -> x6, waiting for transfers between devices: none -> 600 us  [gather_half(): lax.all_gather(piece, ('segment', 'tok'), axis_index_groups=groups, tiled...]
    psum x6 -> x0, waiting for transfers between devices: 313 us -> none  [the longest x3 184 us: spread_2(): return lax.psum(block, axis)]
    dot_general x67 -> x0, matrix products: 117 us -> none  [the longest x42 68.4 us: project(): jnp.einsum('gtd,de->gte', tensor, weight, preferred_element_type=jnp.floa...]
    reshape x50 -> x2, local copies, waits for them, and re-layouts: 49.3 us -> 0.2 us  [the longest x1 0.11 us: send_points(): feats = point_feats.reshape(SECTIONS * TILES, SLOTS * CHANNELS)]
    mul x39 -> x1, local copies, waits for them, and re-layouts: 46.6 us -> 0.08 us  [local(): jnp.tile(all_gains[:, 1024:1088], (1, HEADS)) * 0.125]
    ppermute x35 -> x30, starting transfers between devices: 106 us -> 62.4 us  [the longest x24 62.4 us: with_halo(): blocks.append(lax.ppermute(block, 'tok', route))]
    pallas_call x0 -> x4, Pallas kernels: none -> 41.2 us  [the longest x3 39.2 us: frame(): pl.pallas_call(functools.partial(frame_kernel, with_next), out_shape=out_...]
    all_to_all x0 -> x3, blocking collectives: none -> 41.1 us  [the longest x1 22.7 us: send_points(): lax.all_to_all(message, ('segment', 'tok'), split_axis=0, concat_axis=0,...]
  transfers between devices with their start and end apart: 43 -> 38, of which waited for: 26 -> 13; matrix products, arithmetic and copies ran while one was open for 4% -> 1% of each run, Pallas kernels for 0% -> 2%
where the time goes in v1:
time: 806 us; the launch traced here: 801 us
  waiting for transfers between devices  614 us (76%)
  starting transfers between devices  71.5 us (9%)
  Pallas kernels  41.2 us (5%)
  blocking collectives  41.1 us (5%)
  local copies, waits for them, and re-layouts  16.4 us (2%)
  between operations  14.2 us (2%)
    all_gather x6, waiting for transfers between devices, gather_half(): lax.all_gather(piece, ('segment', 'tok'), axis_index_groups=groups, tiled...  600 us
    ppermute x24, starting transfers between devices, with_halo(): blocks.append(lax.ppermute(block, 'tok', route))  62.4 us
    pallas_call x3, Pallas kernels, frame(): pl.pallas_call(functools.partial(frame_kernel, with_next), out_shape=out_...  39.2 us
    all_to_all x1, blocking collectives, send_points(): lax.all_to_all(message, ('segment', 'tok'), split_axis=0, concat_axis=0,...  22.7 us
  transfers between devices with their start and end apart: 38, of which 13 were waited for; matrix products, arithmetic and copies ran while one was open for 1% of the time, Pallas kernels for 2%

profile of v1, /device:TPU:8, one launch (start us, length us, event | category | flops | bytes accessed | tf_op | source)
XLA Modules:
  0.0 800.9 jit_solution(8310862442732958958)
XLA Ops:
  6.6 1.5 copy-done
  8.9 1.4 constant_dynamic-slice_fusion
  10.4 1.4 constant_dynamic-slice_fusion.3
  11.8 1.3 dynamic_slice.26
  13.2 1.3 constant_dynamic-slice_fusion.2
  14.6 116.7 %all-gather.19.cloned.1.call-done = bf16[1,2048,1024]{2,1,0:T(8,128)(2,1)} async-done(((bf16[1,16,1024]{2,1,0:T(8,128)(2,1)}), bf16[1,2048,1024]{2,1,0:T(8,128)(2,1)}) %all-gather.19.cloned.1.call-update) | async-done | bytes 4194320 | tf_op jit(solution)/shard_map/all_gather | solution.py:272
  131.3 117.7 %all-gather.21.cloned.1.call-done = bf16[1,8192,256]{2,1,0:T(8,128)(2,1)} async-done(((bf16[1,64,256]{2,1,0:T(8,128)(2,1)}), bf16[1,8192,256]{2,1,0:T(8,128)(2,1)}) %all-gather.21.cloned.1.call-update) | async-done | bytes 4194320 | tf_op jit(solution)/shard_map/all_gather | solution.py:272
  249.0 1.3 dynamic_slice.35
  250.3 114.1 %all-gather.15.cloned.1.call-done = bf16[1,2048,768]{2,1,0:T(8,128)(2,1)} async-done(((bf16[1,16,768]{2,1,0:T(8,128)(2,1)}), bf16[1,2048,768]{2,1,0:T(8,128)(2,1)}) %all-gather.15.cloned.1.call-update) | async-done | bytes 3145744 | tf_op jit(solution)/shard_map/all_gather | solution.py:272
  364.4 103.0 %all-gather.11.cloned.1.call-done.mine_ref.refs_16_ = bf16[2048,256]{1,0:T(8,128)(2,1)} async-done(((bf16[16,256]{1,0:T(8,128)(2,1)}), bf16[2048,256]{1,0:T(8,128)(2,1)}) %all-gather.11.cloned.1.call-update) | async-done | bytes 1048592 | tf_op jit(solution)/shard_map/all_gather | solution.py:272
  468.8 1.3 reduce.4
  471.5 22.7 %all_to_all.35 = bf16[256,1,128]{2,1,0:T(2,128)(2,1)S(1)} all-to-all(bf16[256,1,128]{2,1,0:T(2,128)(2,1)S(1)} %copy.26), channel_id=1, replica_groups=mesh['segment'=4,'tok'=64] {'segment','tok'}, dimensions={0} | all-to-all | bytes 131072 | tf_op jit(solution)/shard_map/all_to_all | solution.py:296
  494.3 1.6 copy-done.1
  496.6 2.0 scatter.1
  498.6 3.5 collective-permute-start.1
  502.1 3.0 collective-permute-start.2
  505.2 3.4 collective-permute-start.3
  508.6 2.6 collective-permute-start.4
  511.3 7.9 all_to_all.36
  519.2 1.9 collective-permute-start.5
  521.1 1.9 collective-permute-start.6
  524.4 2.4 collective-permute-done.6
  528.3 44.0 %all-gather.17.cloned.1.call-done = bf16[1,2048,256]{2,1,0:T(8,128)(2,1)} async-done(((bf16[1,16,256]{2,1,0:T(8,128)(2,1)}), bf16[1,2048,256]{2,1,0:T(8,128)(2,1)}) %all-gather.17.cloned.1.call-update) | async-done | bytes 1048592 | tf_op jit(solution)/shard_map/all_gather | solution.py:272
  572.3 104.8 %all-gather.13.cloned.1.call-done.refs_14_ = bf16[2048,256]{1,0:T(8,128)(2,1)} async-done(((bf16[16,256]{1,0:T(8,128)(2,1)}), bf16[2048,256]{1,0:T(8,128)(2,1)}) %all-gather.13.cloned.1.call-update) | async-done | bytes 1048592 | tf_op jit(solution)/shard_map/all_gather | solution.py:272
  677.2 2.7 collective-permute-done.13.refs_15_
  682.2 13.2 %frame.3 = (bf16[4,16,512]{2,1,0:T(8,128)(2,1)}, bf16[16,512]{1,0:T(8,128)(2,1)S(1)}) custom-call(s32[1]{0:T(128)} %bitcast.tile_ref.refs_0_, bf16[144,512]{1,0:T(8,128)(2,1)S(1)} %constant_dynamic-update-slice_fusion.refs_1_, f32[8,512]{1,0:T(8,128)S(1)} %get-tuple-element.19.refs_2_, f32[8,512]{1,0:T(8,128)S(1)} %get-tuple-element.20.refs_3_, ...), custom_call_target="tpu_custom_call" | custom-call | tf_op jit(solution)/shard_map/frame/pallas_call | solution.py:175
  695.4 4.0 collective-permute-start.14
  699.4 2.1 collective-permute-start.15
  701.6 4.0 collective-permute-start.16
  705.6 3.2 collective-permute-start.17
  708.8 2.4 collective-permute-start.18
  711.2 1.9 collective-permute-start.19
  714.4 1.5 collective-permute-start.21
  716.9 1.4 collective-permute-done.20
  718.3 4.0 collective-permute-done.21
  722.3 13.3 %frame.4 = (bf16[4,16,512]{2,1,0:T(8,128)(2,1)}, bf16[16,512]{1,0:T(8,128)(2,1)S(1)}) custom-call(s32[1]{0:T(128)} %bitcast.tile_ref.refs_0_, bf16[144,512]{1,0:T(8,128)(2,1)S(1)} %constant_dynamic-update-slice_fusion.9.refs_1_, f32[8,512]{1,0:T(8,128)S(1)} %get-tuple-element.19.refs_2_, f32[8,512]{1,0:T(8,128)S(1)} %get-tuple-element.20.refs_3_, ...), custom_call_target="tpu_custom_call" | custom-call | tf_op jit(solution)/shard_map/frame/pallas_call | solution.py:175
  735.6 6.3 collective-permute-start.22
  742.0 4.0 all-to-all-start.2
  746.0 2.9 collective-permute-start.23
  748.9 2.9 collective-permute-start.24
  751.8 4.6 collective-permute-start.25
  756.4 1.9 collective-permute-start.26
  758.3 1.9 collective-permute-start.27
  761.6 1.3 collective-permute-start.29
  763.9 1.5 collective-permute-done.28
  765.4 4.8 all-to-all-start.3
  770.2 12.6 %frame.5 = bf16[4,16,512]{2,1,0:T(8,128)(2,1)S(1)} custom-call(s32[1]{0:T(128)} %bitcast.tile_ref.refs_0_, bf16[144,512]{1,0:T(8,128)(2,1)S(1)} %constant_dynamic-update-slice_fusion.18.refs_1_, f32[8,512]{1,0:T(8,128)S(1)} %get-tuple-element.19.refs_2_, f32[8,512]{1,0:T(8,128)S(1)} %get-tuple-element.20.refs_3_, f32[1,512]{1,0:T(1,128)S(1)} %bitcast.33, ...), custom_call_target="tpu_custom_call" | custom-call | tf_op jit(solution)/shard_map/frame/pallas_call | solution.py:175
  782.8 10.5 %all_to_all.37 = bf16[4,16,512]{2,1,0:T(8,128)(2,1)S(1)} all-to-all(bf16[4,16,512]{2,1,0:T(8,128)(2,1)S(1)} %frame.5), channel_id=1, replica_groups=mesh['segment'=4,'tok'=64] {'segment'}, dimensions={0} | all-to-all | bytes 131072 | tf_op jit(solution)/shard_map/all_to_all | solution.py:355
  (125 shorter events, 14.9 us)
Async XLA Ops:
  6.5 1.7 copy-start
  6.5 674.4 %copy-start.6 = (f32[512]{0:T(512)S(1)}, f32[512]{0:T(512)}, u32[]{:S(2)}) copy-start(f32[512]{0:T(512)} %param.19) | copy-start | bytes 6148
  6.5 504.6 %copy-start.9 = (f32[1,512]{1,0:T(1,128)S(1)}, f32[1,512]{1,0:T(1,128)}, u32[]{:S(2)}) copy-start(f32[1,512]{1,0:T(1,128)} %param.22) | copy-start | bytes 6148
  6.5 504.6 %copy-start.10 = (f32[1,512]{1,0:T(1,128)S(1)}, f32[1,512]{1,0:T(1,128)}, u32[]{:S(2)}) copy-start(f32[1,512]{1,0:T(1,128)} %param.23) | copy-start | bytes 6148
  6.5 504.6 %copy-start.11 = (f32[1,64]{1,0:T(1,128)S(1)}, f32[1,64]{1,0:T(1,128)}, u32[]{:S(2)}) copy-start(f32[1,64]{1,0:T(1,128)} %param.24) | copy-start | bytes 772
  6.5 504.6 %copy-start.12 = (f32[1,64]{1,0:T(1,128)S(1)}, f32[1,64]{1,0:T(1,128)}, u32[]{:S(2)}) copy-start(f32[1,64]{1,0:T(1,128)} %param.25) | copy-start | bytes 772
  6.6 674.4 %copy-start.7 = (f32[512]{0:T(512)S(1)}, f32[512]{0:T(512)}, u32[]{:S(2)}) copy-start(f32[512]{0:T(512)} %param.21) | copy-start | bytes 6148
  6.6 124.7 %all-gather.19.cloned.1.call-start = ((), (), s32[]{:S(2)}) async-start(), calls=%async_computation.9 | async-start | bytes 4227072 | tf_op jit(solution)/shard_map/all_gather | solution.py:272
  8.8 240.1 %all-gather.21.cloned.1.call-start = ((), (), s32[]{:S(2)}) async-start(), calls=%async_computation.10 | async-start | bytes 4227072 | tf_op jit(solution)/shard_map/all_gather | solution.py:272
  10.3 354.1 %all-gather.15.cloned.1.call-start = ((), (), s32[]{:S(2)}) async-start(), calls=%async_computation.7 | async-start | bytes 3170304 | tf_op jit(solution)/shard_map/all_gather | solution.py:272
  11.8 455.7 %all-gather.11.cloned.1.call-start = ((), (), s32[]{:S(2)}) async-start(), calls=%async_computation.5 | async-start | bytes 1056768 | tf_op jit(solution)/shard_map/all_gather | solution.py:272
  13.1 559.2 %all-gather.17.cloned.1.call-start = ((), (), s32[]{:S(2)}) async-start(), calls=%async_computation.8 | async-start | bytes 1056768 | tf_op jit(solution)/shard_map/all_gather | solution.py:272
  14.5 662.5 %all-gather.13.cloned.1.call-start = ((), (), s32[]{:S(2)}) async-start(), calls=%async_computation.6 | async-start | bytes 1056768 | tf_op jit(solution)/shard_map/all_gather | solution.py:272
  131.3 548.7 %collective-permute-start.11 = (bf16[2048,1024]{1,0:T(8,128)(2,1)}, bf16[2048,1024]{1,0:T(8,128)(2,1)}, u32[]{:S(2)}, u32[]{:S(2)}) collective-permute-start(bf16[2048,1024]{1,0:T(8,128)(2,1)} %bitcast.34), channel_id=1, source_target_pairs={{0,1},{1,0},{2,3},{3,2},{4,5},{5,4},{6,7},{7,6},{8,9},{9,8},{10,11... | collective-permute-start | bytes 12582920 | tf_op jit(solution)/shard_map/ppermute | solution.py:259
  249.0 431.0 %collective-permute-start.12 = (bf16[8192,256]{1,0:T(8,128)(2,1)}, bf16[8192,256]{1,0:T(8,128)(2,1)}, u32[]{:S(2)}, u32[]{:S(2)}) collective-permute-start(bf16[8192,256]{1,0:T(8,128)(2,1)} %bitcast.38), channel_id=1, source_target_pairs={{0,1},{1,0},{2,3},{3,2},{4,5},{5,4},{6,7},{7,6},{8,9},{9,8},{10,11... | collective-permute-start | bytes 12582920 | tf_op jit(solution)/shard_map/ppermute | solution.py:259
  364.4 315.5 %collective-permute-start.9 = (bf16[2048,768]{1,0:T(8,128)(2,1)}, bf16[2048,768]{1,0:T(8,128)(2,1)}, u32[]{:S(2)}, u32[]{:S(2)}) collective-permute-start(bf16[2048,768]{1,0:T(8,128)(2,1)} %bitcast.42), channel_id=1, source_target_pairs={{0,1},{1,0},{2,3},{3,2},{4,5},{5,4},{6,7},{7,6},{8,9},{9,8},{10,11... | collective-permute-start | bytes 9437192 | tf_op jit(solution)/shard_map/ppermute | solution.py:259
  467.5 26.8 %collective-permute-start = (bf16[2048,256]{1,0:T(8,128)(2,1)}, bf16[2048,256]{1,0:T(8,128)(2,1)S(1)}, u32[]{:S(2)}, u32[]{:S(2)}) collective-permute-start(bf16[2048,256]{1,0:T(8,128)(2,1)} %all-gather.11.cloned.1.call-done.mine_ref.refs_16_), channel_id=1, source_target_pairs={{0,1},{1,0},{2,3},{3,2},{4,5},{5,4},{6,7},{7,6},{8,9},{9,8},{10,11... | collective-permute-start | bytes 3145736 | tf_op jit(solution)/shard_map/ppermute | solution.py:259
  494.3 185.7 %copy-start.2 = (bf16[2048,256]{1,0:T(8,128)(2,1)}, bf16[2048,256]{1,0:T(8,128)(2,1)S(1)}, u32[]{:S(2)}) copy-start(bf16[2048,256]{1,0:T(8,128)(2,1)S(1)} %collective-permute-done.other_ref.refs_17_) | copy-start | bytes 3145732
  494.3 1.6 copy-start.1
  498.6 6.6 collective-permute-start.1
  502.1 6.4 collective-permute-start.2
  505.2 14.0 %collective-permute-start.3 = (bf16[16,512]{1,0:T(8,128)(2,1)S(1)}, bf16[16,512]{1,0:T(8,128)(2,1)S(1)}, u32[]{:S(2)}, u32[]{:S(2)}) collective-permute-start(bf16[16,512]{1,0:T(8,128)(2,1)S(1)} %scatter.1), channel_id=1, source_target_pairs={{0,2},{1,3},{2,4},{3,5},{4,6},{5,7},{6,8},{7,9},{8,10},{9,11},{10,... | collective-permute-start | bytes 49160 | tf_op jit(solution)/shard_map/ppermute | solution.py:282
  508.6 12.5 %collective-permute-start.4 = (bf16[16,512]{1,0:T(8,128)(2,1)S(1)}, bf16[16,512]{1,0:T(8,128)(2,1)S(1)}, u32[]{:S(2)}, u32[]{:S(2)}) collective-permute-start(bf16[16,512]{1,0:T(8,128)(2,1)S(1)} %scatter.1), channel_id=1, source_target_pairs={{0,1},{1,2},{2,3},{3,4},{4,5},{5,6},{6,7},{7,8},{8,9},{9,10},{10,1... | collective-permute-start | bytes 49160 | tf_op jit(solution)/shard_map/ppermute | solution.py:282
  519.2 3.9 collective-permute-start.5
  521.1 5.6 collective-permute-start.6
  523.1 49.2 %collective-permute-start.7 = (bf16[16,512]{1,0:T(8,128)(2,1)S(1)}, bf16[16,512]{1,0:T(8,128)(2,1)S(1)}, u32[]{:S(2)}, u32[]{:S(2)}) collective-permute-start(bf16[16,512]{1,0:T(8,128)(2,1)S(1)} %scatter.1), channel_id=1, source_target_pairs={{3,0},{4,1},{5,2},{6,3},{7,4},{8,5},{9,6},{10,7},{11,8},{12,9},{13... | collective-permute-start | bytes 49160 | tf_op jit(solution)/shard_map/ppermute | solution.py:282
  526.7 150.3 %collective-permute-start.8 = (bf16[16,512]{1,0:T(8,128)(2,1)S(1)}, bf16[16,512]{1,0:T(8,128)(2,1)S(1)}, u32[]{:S(2)}, u32[]{:S(2)}) collective-permute-start(bf16[16,512]{1,0:T(8,128)(2,1)S(1)} %scatter.1), channel_id=1, source_target_pairs={{4,0},{5,1},{6,2},{7,3},{8,4},{9,5},{10,6},{11,7},{12,8},{13,9},{1... | collective-permute-start | bytes 49160 | tf_op jit(solution)/shard_map/ppermute | solution.py:282
  572.3 104.9 %collective-permute-start.10 = (bf16[2048,256]{1,0:T(8,128)(2,1)}, bf16[2048,256]{1,0:T(8,128)(2,1)}, u32[]{:S(2)}, u32[]{:S(2)}) collective-permute-start(bf16[2048,256]{1,0:T(8,128)(2,1)} %bitcast.22), channel_id=1, source_target_pairs={{0,1},{1,0},{2,3},{3,2},{4,5},{5,4},{6,7},{7,6},{8,9},{9,8},{10,11... | collective-permute-start | bytes 3145736 | tf_op jit(solution)/shard_map/ppermute | solution.py:259
  677.1 2.9 collective-permute-start.13
  695.4 15.7 %collective-permute-start.14 = (bf16[16,512]{1,0:T(8,128)(2,1)S(1)}, bf16[16,512]{1,0:T(8,128)(2,1)S(1)}, u32[]{:S(2)}, u32[]{:S(2)}) collective-permute-start(bf16[16,512]{1,0:T(8,128)(2,1)S(1)} %get-tuple-element.10), channel_id=1, source_target_pairs={{0,4},{1,5},{2,6},{3,7},{4,8},{5,9},{6,10},{7,11},{8,12},{9,13},{1... | collective-permute-start | bytes 49160 | tf_op jit(solution)/shard_map/ppermute | solution.py:282
  699.4 13.7 %collective-permute-start.15 = (bf16[16,512]{1,0:T(8,128)(2,1)S(1)}, bf16[16,512]{1,0:T(8,128)(2,1)S(1)}, u32[]{:S(2)}, u32[]{:S(2)}) collective-permute-start(bf16[16,512]{1,0:T(8,128)(2,1)S(1)} %get-tuple-element.10), channel_id=1, source_target_pairs={{0,3},{1,4},{2,5},{3,6},{4,7},{5,8},{6,9},{7,10},{8,11},{9,12},{10... | collective-permute-start | bytes 49160 | tf_op jit(solution)/shard_map/ppermute | solution.py:282
  701.6 12.9 %collective-permute-start.16 = (bf16[16,512]{1,0:T(8,128)(2,1)S(1)}, bf16[16,512]{1,0:T(8,128)(2,1)S(1)}, u32[]{:S(2)}, u32[]{:S(2)}) collective-permute-start(bf16[16,512]{1,0:T(8,128)(2,1)S(1)} %get-tuple-element.10), channel_id=1, source_target_pairs={{0,2},{1,3},{2,4},{3,5},{4,6},{5,7},{6,8},{7,9},{8,10},{9,11},{10,... | collective-permute-start | bytes 49160 | tf_op jit(solution)/shard_map/ppermute | solution.py:282
  705.6 10.4 %collective-permute-start.17 = (bf16[16,512]{1,0:T(8,128)(2,1)S(1)}, bf16[16,512]{1,0:T(8,128)(2,1)S(1)}, u32[]{:S(2)}, u32[]{:S(2)}) collective-permute-start(bf16[16,512]{1,0:T(8,128)(2,1)S(1)} %get-tuple-element.10), channel_id=1, source_target_pairs={{0,1},{1,2},{2,3},{3,4},{4,5},{5,6},{6,7},{7,8},{8,9},{9,10},{10,1... | collective-permute-start | bytes 49160 | tf_op jit(solution)/shard_map/ppermute | solution.py:282
  708.8 7.2 collective-permute-start.18
  711.2 5.7 collective-permute-start.19
  713.1 5.1 collective-permute-start.20
  714.4 7.8 collective-permute-start.21
  722.3 47.9 %copy-start.4 = (bf16[1,2048,256]{2,1,0:T(8,128)(2,1)S(1)}, bf16[1,2048,256]{2,1,0:T(8,128)(2,1)}, u32[]{:S(2)}) copy-start(bf16[1,2048,256]{2,1,0:T(8,128)(2,1)} %all-gather.17.cloned.1.call-done) | copy-start | bytes 3145732
  735.6 22.7 %collective-permute-start.22 = (bf16[16,512]{1,0:T(8,128)(2,1)S(1)}, bf16[16,512]{1,0:T(8,128)(2,1)S(1)}, u32[]{:S(2)}, u32[]{:S(2)}) collective-permute-start(bf16[16,512]{1,0:T(8,128)(2,1)S(1)} %get-tuple-element.12), channel_id=1, source_target_pairs={{0,4},{1,5},{2,6},{3,7},{4,8},{5,9},{6,10},{7,11},{8,12},{9,13},{1... | collective-permute-start | bytes 49160 | tf_op jit(solution)/shard_map/ppermute | solution.py:282
  742.0 23.5 %all-to-all-start.2 = ((bf16[4,16,512]{2,1,0:T(8,128)(2,1)}), bf16[4,16,512]{2,1,0:T(8,128)(2,1)S(1)}, u32[]{:S(2)}, u32[]{:S(2)}) async-start(bf16[4,16,512]{2,1,0:T(8,128)(2,1)} %get-tuple-element.9), calls=%async_computation.2 | async-start | bytes 131072 | tf_op jit(solution)/shard_map/all_to_all | solution.py:355
  746.0 14.3 %collective-permute-start.23 = (bf16[16,512]{1,0:T(8,128)(2,1)S(1)}, bf16[16,512]{1,0:T(8,128)(2,1)S(1)}, u32[]{:S(2)}, u32[]{:S(2)}) collective-permute-start(bf16[16,512]{1,0:T(8,128)(2,1)S(1)} %get-tuple-element.12), channel_id=1, source_target_pairs={{0,3},{1,4},{2,5},{3,6},{4,7},{5,8},{6,9},{7,10},{8,11},{9,12},{10... | collective-permute-start | bytes 49160 | tf_op jit(solution)/shard_map/ppermute | solution.py:282
  748.9 12.7 %collective-permute-start.24 = (bf16[16,512]{1,0:T(8,128)(2,1)S(1)}, bf16[16,512]{1,0:T(8,128)(2,1)S(1)}, u32[]{:S(2)}, u32[]{:S(2)}) collective-permute-start(bf16[16,512]{1,0:T(8,128)(2,1)S(1)} %get-tuple-element.12), channel_id=1, source_target_pairs={{0,2},{1,3},{2,4},{3,5},{4,6},{5,7},{6,8},{7,9},{8,10},{9,11},{10,... | collective-permute-start | bytes 49160 | tf_op jit(solution)/shard_map/ppermute | solution.py:282
  751.8 11.1 %collective-permute-start.25 = (bf16[16,512]{1,0:T(8,128)(2,1)S(1)}, bf16[16,512]{1,0:T(8,128)(2,1)S(1)}, u32[]{:S(2)}, u32[]{:S(2)}) collective-permute-start(bf16[16,512]{1,0:T(8,128)(2,1)S(1)} %get-tuple-element.12), channel_id=1, source_target_pairs={{0,1},{1,2},{2,3},{3,4},{4,5},{5,6},{6,7},{7,8},{8,9},{9,10},{10,1... | collective-permute-start | bytes 49160 | tf_op jit(solution)/shard_map/ppermute | solution.py:282
  756.4 6.6 collective-permute-start.26
  758.3 5.6 collective-permute-start.27
  760.2 5.2 collective-permute-start.28
  761.6 8.6 %collective-permute-start.29 = (bf16[16,512]{1,0:T(8,128)(2,1)S(1)}, bf16[16,512]{1,0:T(8,128)(2,1)S(1)}, u32[]{:S(2)}, u32[]{:S(2)}) collective-permute-start(bf16[16,512]{1,0:T(8,128)(2,1)S(1)} %get-tuple-element.12), channel_id=1, source_target_pairs={{4,0},{5,1},{6,2},{7,3},{8,4},{9,5},{10,6},{11,7},{12,8},{13,9},{1... | collective-permute-start | bytes 49160 | tf_op jit(solution)/shard_map/ppermute | solution.py:282
  765.4 17.4 %all-to-all-start.3 = ((bf16[4,16,512]{2,1,0:T(8,128)(2,1)}), bf16[4,16,512]{2,1,0:T(8,128)(2,1)S(1)}, u32[]{:S(2)}, u32[]{:S(2)}) async-start(bf16[4,16,512]{2,1,0:T(8,128)(2,1)} %get-tuple-element.11), calls=%async_computation.3 | async-start | bytes 131072 | tf_op jit(solution)/shard_map/all_to_all | solution.py:355
  (3 other events, 2.9 us)
Sparse Core Ops, SparseCore 0:
  11.0 120.1 all-gather.18
  134.9 114.0 all-gather.20
  252.6 111.7 all-gather.14
  367.7 99.7 all-gather.10
  470.7 101.5 all-gather.16
  575.6 101.4 all-gather.12
